TPU v7x, 512 devices: a whole 4x4x16 slice. The times are simulated.
512 devices in a mesh: dom: 64 (over x, z), head: 8 (over y, core).
Axes of the slice: x: 4, y: 4, z: 16, core: 2. Of those that a mesh axis runs over, the one named last changes fastest.
Arguments:
- node_feats: bfloat16 [65536, 512], P(('dom', 'head')), may hold values from -6 to 6
- norm_gain: float32 [512], replicated, may hold values from 0.25 to 1.75
- w_qkv: bfloat16 [512, 1536], P(None, 'head'), may hold values from -1 to 1
- w_out: bfloat16 [512, 512], replicated, may hold values from -0.25 to 0.25
- rand_feat: float32 [8, 64, 256], P('head'), may hold values from -6 to 6
- temper: float32 [8], P('head'), may hold values from 1 to 6
- edge_src: int32 [512, 6], P('dom'), may hold values from 0 to 511, as said below
- edge_count: int32 [512], P('dom'), may hold values from 1 to 6, as said below
- block_fill: int32 [512], replicated, may hold values from 32 to 128, as said below
Outputs:
- update: bfloat16 [65536, 512], P(('dom', 'head'))
Inputs may be any that keep to these rules, and one draw needn't show every extreme that they name: `edge_src`: destination block b lies in partition p = b // 8; each of its source blocks lies in partition p - 1, p or p + 1; slot 0 holds b itself, and slots at or beyond edge_count[b] hold b. `edge_count`: every block of some partition uses all 6 slots. `block_fill`: block 0 is full.
All inputs are finite; a program needn't handle non-finite values.
Results may differ from a plain program's by a relative error of at most 0.012.
The roundings to bfloat16 on the way count: a program that leaves them out, or rounds other values in their place, can miss the bound.
Values may be sent and summed in bfloat16 or wider, within the bound.
A program may use at most 64 MiB of HBM per device.

v0:
```python
import math
import jax
import jax.numpy as jnp
from jax import lax
from jax.sharding import PartitionSpec as P

BLK = 128


def padded(block, sides, width):
    for axis, dim in sides:
        count = lax.axis_size(axis)
        forward = [(i, i + 1) for i in range(count - 1)]
        backward = [(target, source) for source, target in forward]
        low = lax.ppermute(
            lax.slice_in_dim(block, block.shape[dim] - width, None, axis=dim), axis, forward
        )
        high = lax.ppermute(lax.slice_in_dim(block, 0, width, axis=dim), axis, backward)
        block = jnp.concatenate([low, block, high], axis=dim)
    return block


def layer_norm(rows, gain):
    widened = rows.astype(jnp.float32)
    centred = widened - jnp.mean(widened, axis=-1, keepdims=True)
    spread = jnp.mean(centred * centred, axis=-1, keepdims=True)
    return (centred * lax.rsqrt(spread + 1e-05) * gain).astype(jnp.bfloat16)


def features(rows, directions, temper):
    head_dim = rows.shape[-1]
    scaled = rows.astype(jnp.float32) * (jnp.sqrt(temper)[None, :, None] * head_dim ** (-0.25))
    lifted = jnp.einsum("nhd,hdm->nhm", scaled, directions, precision=lax.Precision.HIGHEST)
    return jnp.exp(
        lifted - 0.5 * jnp.sum(scaled * scaled, axis=-1, keepdims=True)
    ) * directions.shape[2] ** (-0.5)


def shards(
    node_feats, norm_gain, w_qkv, w_out, rand_feat, temper, edge_src, edge_count, block_fill
):
    groups = lax.axis_size("head")
    heads_here = rand_feat.shape[0]
    head_dim = rand_feat.shape[1]
    part_rows = node_feats.shape[0] * groups
    blocks = part_rows // BLK
    slots = edge_src.shape[1]
    domain = lax.axis_index("dom")
    normed = layer_norm(node_feats, norm_gain)
    qkv = jnp.dot(
        lax.all_gather(normed, "head", axis=0, tiled=True),
        w_qkv,
        preferred_element_type=jnp.float32,
    ).astype(jnp.bfloat16)
    split = qkv.reshape(part_rows, heads_here, 3, head_dim)
    queries = split[:, :, 0]
    own_fill = lax.dynamic_slice_in_dim(block_fill, domain * blocks, blocks)
    lanes = lax.broadcasted_iota(jnp.int32, (blocks, BLK), 1)
    valid = (lanes < own_fill[:, None]).astype(jnp.float32).reshape(part_rows)
    phi_keys = features(split[:, :, 1], rand_feat, temper) * valid[:, None, None]
    partial_sum = jnp.einsum(
        "nhm,nhe->hme",
        phi_keys,
        split[:, :, 2].astype(jnp.float32),
        precision=lax.Precision.HIGHEST,
    )
    kernel_sum, key_total = lax.psum((partial_sum, jnp.sum(phi_keys, axis=0)), "dom")
    pairs = split[:, :, 1:].reshape(part_rows, heads_here * 2 * head_dim)
    widened = padded(pairs, (("dom", 0),), part_rows)
    kv_blocks = widened.reshape(3 * blocks, BLK, heads_here, 2, head_dim)
    key_blocks = kv_blocks[:, :, :, 0]
    value_blocks = kv_blocks[:, :, :, 1]
    local_src = edge_src - (domain - 1) * blocks
    scale = head_dim ** (-0.5)
    per_step = math.gcd(blocks, max(1, 8 // heads_here))
    turns = blocks // per_step
    width = slots * BLK
    q_steps = queries.reshape(turns, per_step, BLK, heads_here, head_dim)
    src_steps = local_src.reshape(turns, per_step, slots)
    id_steps = edge_src.reshape(turns, per_step, slots)
    count_steps = edge_count.reshape(turns, per_step)

    def attend_all(packed):
        q_part, src_part, id_part, count_part = packed
        keys = jnp.take(key_blocks, src_part, axis=0).reshape(per_step, width, heads_here, head_dim)
        values = jnp.take(value_blocks, src_part, axis=0).reshape(
            per_step, width, heads_here, head_dim
        )
        fills = jnp.take(block_fill, id_part)
        slot_ids = lax.broadcasted_iota(jnp.int32, (per_step, slots, BLK), 1)
        lane_ids = lax.broadcasted_iota(jnp.int32, (per_step, slots, BLK), 2)
        allowed = ((lane_ids < fills[:, :, None]) & (slot_ids < count_part[:, None, None])).reshape(
            per_step, width
        )
        scores = (
            jnp.einsum("bqhd,bkhd->bhqk", q_part, keys, preferred_element_type=jnp.float32) * scale
        )
        scores = jnp.where(allowed[:, None, None, :], scores, -1e30)
        row_max = jnp.max(scores, axis=3, keepdims=True)
        weights = jnp.exp(scores - row_max)
        total = jnp.sum(weights, axis=3)
        accum = jnp.einsum(
            "bhqk,bkhd->bqhd",
            weights.astype(jnp.bfloat16),
            values,
            preferred_element_type=jnp.float32,
        )
        return accum / jnp.transpose(total, (0, 2, 1))[..., None]

    local = lax.map(attend_all, (q_steps, src_steps, id_steps, count_steps))
    local = local.reshape(part_rows, heads_here, head_dim)
    phi_queries = features(queries, rand_feat, temper)
    numer = jnp.einsum("nhm,hme->nhe", phi_queries, kernel_sum, precision=lax.Precision.HIGHEST)
    denom = jnp.einsum("nhm,hm->nh", phi_queries, key_total, precision=lax.Precision.HIGHEST)
    mixed = (
        (local + numer / denom[..., None])
        .astype(jnp.bfloat16)
        .reshape(part_rows, heads_here * head_dim)
    )
    returned = lax.all_to_all(mixed, "head", split_axis=0, concat_axis=1, tiled=True)
    return jnp.dot(returned, w_out, preferred_element_type=jnp.float32).astype(jnp.bfloat16)


def solution(mesh):
    return jax.shard_map(
        shards,
        mesh=mesh,
        in_specs=(
            P(("dom", "head"), None),
            P(),
            P(None, "head"),
            P(),
            P("head", None, None),
            P("head"),
            P("dom", None),
            P("dom"),
            P(),
        ),
        out_specs=P(("dom", "head"), None),
        check_vma=False,
    )
```

profile of v0, /device:TPU:1, one launch (start us, length us, event | category | flops | bytes accessed | tf_op | source)
XLA Modules:
  0.0 337.9 jit_solution(1613953993842794324)
XLA Ops:
  6.5 0.0 copy-start
  6.5 0.0 copy-start.6
  6.5 0.0 copy-start.1
  6.5 0.0 copy-start.5
  6.5 0.0 all-gather.2.cloned.1.call-start
  6.6 1.1 convert_reduce_fusion
  7.7 1.1 fusion.31
  8.8 1.7 fusion.33
  10.5 0.0 all-gather.2.cloned.1.call-update
  10.5 0.0 all-reduce.2.cloned.1.call-start
  10.6 1.3 compare_and_fusion
  11.8 0.1 reshape.313
  11.9 0.7 compare_select_fusion.1
  12.6 0.1 reshape.298
  12.7 0.0 copy-done.1
  12.7 0.0 copy-start.4
  12.7 0.8 gather_fusion
  13.5 0.1 reshape.297
  13.6 0.0 copy-done.6
  13.6 0.1 copy.20
  14.4 0.1 dynamic_slice.14
  14.5 0.1 select_bitcast_fusion
  14.6 0.0 copy-done.7
  14.6 0.1 fusion.44
  14.6 33.0 %all-gather.2.cloned.1.call-done = bf16[1024,512]{1,0:T(8,128)(2,1)} async-done(((bf16[128,512]{1,0:T(8,128)(2,1)}), bf16[1024,512]{1,0:T(8,128)(2,1)}) %all-gather.2.cloned.1.call-update) | async-done | bytes 1048592 | tf_op jit(solution)/shard_map/all_gather | solution.py:51
  47.6 0.0 copy-done.5
  47.6 1.7 convolution_convert_fusion
  49.4 3.0 collective-permute-start
  52.4 1.3 collective-permute-start.1
  53.7 0.1 multiply_reduce_fusion
  53.8 0.0 copy-done.4
  53.9 1.3 fusion.48
  55.1 1.1 fusion.27
  56.2 1.1 fusion.12
  57.4 0.7 copy.30
  58.1 0.0 all-reduce.2.cloned.1.call-update
  58.1 117.4 %psum.15 = f32[256]{0:T(256)S(1)} all-reduce(f32[256]{0:T(256)S(1)} %get-tuple-element.43), channel_id=1, replica_groups=mesh['dom'=64,'head'=8] {'dom'}, use_global_device_ids=true, to_apply=%region_8.10 | all-reduce | flops 256 | bytes 2048 | tf_op jit(solution)/shard_map/psum | solution.py:67
  175.5 1.0 fusion.49
  176.5 0.0 collective-permute-done
  176.5 0.0 collective-permute-done.1
  176.5 0.1 maximum_bitcast_fusion
  176.6 0.2 copy.29
  176.7 0.1 fusion.47
  176.8 0.2 copy_bitcast_fusion
  177.0 0.7 gather_fusion.1
  177.7 0.7 gather_fusion.2
  178.4 1.8 broadcast_select_fusion
  180.2 0.6 copy.22
  180.7 0.0 copy-start.3
  180.7 0.9 reshape.266
  181.6 1.7 copy.19
  183.3 1.8 reshape.264
  185.1 0.0 copy-done.3
  185.1 0.0 copy-start.2
  185.1 0.7 fusion
  185.8 0.9 fusion.1
  186.8 0.0 copy-done.2
  186.8 1.0 fusion.24
  187.7 0.2 copy.24
  187.9 120.0 %all-reduce.2.cloned.1.call-done = f32[256,64]{0,1:T(8,128)} async-done(((f32[256,64]{0,1:T(8,128)}), f32[256,64]{0,1:T(8,128)}) %all-reduce.2.cloned.1.call-update) | async-done | bytes 65552 | tf_op jit(solution)/shard_map/psum | solution.py:67
  307.9 2.0 fusion.20
  309.9 20.3 %all_to_all.19 = bf16[8,128,64]{1,2,0:T(8,128)(2,1)S(1)} all-to-all(bf16[8,128,64]{1,2,0:T(8,128)(2,1)S(1)} %copy.26), channel_id=1, replica_groups=mesh['dom'=64,'head'=8] {'head'}, dimensions={0} | all-to-all | bytes 262144 | tf_op jit(solution)/shard_map/all_to_all | solution.py:120
  330.2 0.0 copy-done
  330.2 0.9 convolution_convert_fusion.1
  (13 shorter events, 0.1 us)
Async XLA Ops:
  6.5 323.6 %copy-start = (bf16[512,512]{1,0:T(8,128)(2,1)S(1)}, bf16[512,512]{1,0:T(8,128)(2,1)}, u32[]{:S(2)}) copy-start(bf16[512,512]{1,0:T(8,128)(2,1)} %param.14) | copy-start | bytes 1572868
  6.5 7.1 %copy-start.6 = (s32[8,6]{1,0:T(8,128)S(1)}, s32[8,6]{1,0:T(8,128)}, u32[]{:S(2)}) copy-start(s32[8,6]{1,0:T(8,128)} %param.17) | copy-start | bytes 580
  6.5 6.2 %copy-start.1 = (s32[512]{0:T(512)S(1)}, s32[512]{0:T(512)}, u32[]{:S(2)}) copy-start(s32[512]{0:T(512)} %param.19) | copy-start | bytes 6148
  6.5 8.0 %copy-start.7 = (s32[8]{0:T(128)S(1)}, s32[8]{0:T(128)}, u32[]{:S(2)}) copy-start(s32[8]{0:T(128)} %param.18) | copy-start | bytes 100
  6.5 41.1 %copy-start.5 = (bf16[512,192]{0,1:T(8,128)(2,1)S(1)}, bf16[512,192]{0,1:T(8,128)(2,1)}, u32[]{:S(2)}) copy-start(bf16[512,192]{0,1:T(8,128)(2,1)} %param.13) | copy-start | bytes 589828
  6.5 41.1 %all-gather.2.cloned.1.call-start = ((), (), s32[]{:S(2)}) async-start(), calls=%async_computation.1 | async-start | bytes 1179648 | tf_op jit(solution)/shard_map/all_gather | solution.py:51
  10.5 297.3 %all-reduce.2.cloned.1.call-start = ((), (), s32[]{:S(2)}) async-start(), calls=%async_computation.2 | async-start | bytes 131072 | tf_op jit(solution)/shard_map/psum | solution.py:67
  12.7 41.1 %copy-start.4 = (f32[1,64,256]{2,1,0:T(8,128)S(1)}, f32[1,64,256]{2,1,0:T(8,128)}, u32[]{:S(2)}) copy-start(f32[1,64,256]{2,1,0:T(8,128)} %param.15) | copy-start | bytes 196612
  49.4 127.1 %collective-permute-start = (bf16[1024,128]{0,1:T(8,128)(2,1)S(1)}, bf16[1024,128]{0,1:T(8,128)(2,1)S(1)}, u32[]{:S(2)}, u32[]{:S(2)}) collective-permute-start(bf16[1024,128]{0,1:T(8,128)(2,1)S(1)} %bitcast.148), channel_id=1, source_target_pairs={{0,8},{8,16},{16,24},{24,32},{32,40},{40,48},{48,56},{56,64},{64,7... | collective-permute-start | bytes 786440 | tf_op jit(solution)/shard_map/ppermute | solution.py:15
  52.4 124.1 %collective-permute-start.1 = (bf16[1024,128]{0,1:T(8,128)(2,1)S(1)}, bf16[1024,128]{0,1:T(8,128)(2,1)S(1)}, u32[]{:S(2)}, u32[]{:S(2)}) collective-permute-start(bf16[1024,128]{0,1:T(8,128)(2,1)S(1)} %bitcast.149), channel_id=1, source_target_pairs={{8,0},{16,8},{24,16},{32,24},{40,32},{48,40},{56,48},{64,56},{72,6... | collective-permute-start | bytes 786440 | tf_op jit(solution)/shard_map/ppermute | solution.py:18
  180.7 4.4 %copy-start.3 = (bf16[8,8,8,128]{3,2,1,0:T(8,128)(2,1)S(1)}, bf16[8,8,8,128]{3,2,1,0:T(8,128)(2,1)}, u32[]{:S(2)}) copy-start(bf16[8,8,8,128]{3,2,1,0:T(8,128)(2,1)} %copy.30) | copy-start | bytes 393220
  185.1 1.6 copy-start.2
Sparse Core Ops, SparseCore 0:
  10.6 36.9 all-gather.1
  58.2 249.6 all-reduce.1
where the time goes:
time: 338 us
  waiting for transfers between devices  153 us (45%)
  blocking collectives  138 us (41%)
  between operations  14.4 us (4%)
  matrix products  10.7 us (3%)
  local copies, waits for them, and re-layouts  8.88 us (3%)
  other arithmetic  8.83 us (3%)
  starting transfers between devices  4.4 us (1%)
    psum x1, waiting for transfers between devices, shards(): lax.psum((partial_sum, jnp.sum(phi_keys, axis=0)), 'dom')  120 us
    psum x1, blocking collectives, shards(): lax.psum((partial_sum, jnp.sum(phi_keys, axis=0)), 'dom')  117 us
    all_gather x1, waiting for transfers between devices, shards(): lax.all_gather(normed, 'head', axis=0, tiled=True)  33 us
    all_to_all x1, blocking collectives, shards(): lax.all_to_all(mixed, 'head', split_axis=0, concat_axis=1, tiled=True)  20.3 us
  transfers between devices with their start and end apart: 4, of which 2 were waited for; matrix products, arithmetic and copies ran while one was open for 6% of the time, Pallas kernels for 0%

commit v1 on v0

--- a/solution.py
+++ b/solution.py
@@ -1,3 +1,4 @@
+import functools
 import math
 import jax
 import jax.numpy as jnp
@@ -5,6 +6,19 @@
 from jax.sharding import PartitionSpec as P
 
 BLK = 128
+
+
+def list_the_windows(load, shard_axis):
+    history = []
+    for _ in range(lax.axis_size(shard_axis)):
+        history.append(load)
+    local_part = jnp.stack(history, 0)
+    z_new = lax.all_to_all(local_part, shard_axis, 0, 0)
+    arr_next = jnp.concatenate(z_new, 0)
+    return arr_next
+
+
+cover_the_series_all = functools.partial(list_the_windows, shard_axis="head")
 
 
 def padded(block, sides, width):
@@ -47,11 +61,9 @@
     slots = edge_src.shape[1]
     domain = lax.axis_index("dom")
     normed = layer_norm(node_feats, norm_gain)
-    qkv = jnp.dot(
-        lax.all_gather(normed, "head", axis=0, tiled=True),
-        w_qkv,
-        preferred_element_type=jnp.float32,
-    ).astype(jnp.bfloat16)
+    qkv = jnp.dot(cover_the_series_all(normed), w_qkv, preferred_element_type=jnp.float32).astype(
+        jnp.bfloat16
+    )
     split = qkv.reshape(part_rows, heads_here, 3, head_dim)
     queries = split[:, :, 0]
     own_fill = lax.dynamic_slice_in_dim(block_fill, domain * blocks, blocks)

time: 338 us -> 325 us (0.962)
  waiting for transfers between devices: 153 us -> 130 us
  starting transfers between devices: 4.4 us -> 13.1 us
    all_gather x1 -> x0, waiting for transfers between devices: 33 us -> none  [shards(): lax.all_gather(normed, 'head', axis=0, tiled=True)]
    all_to_all x0 -> x1, waiting for transfers between devices: none -> 12.4 us  [list_the_windows(): z_new = lax.all_to_all(local_part, shard_axis, 0, 0)]
    all_to_all x0 -> x1, starting transfers between devices: none -> 10.5 us  [list_the_windows(): z_new = lax.all_to_all(local_part, shard_axis, 0, 0)]
where the time goes in v1:
time: 325 us; the launch traced here: 324 us
  blocking collectives  140 us (43%)
  waiting for transfers between devices  130 us (40%)
  between operations  14.4 us (4%)
  starting transfers between devices  13.1 us (4%)
  local copies, waits for them, and re-layouts  9.95 us (3%)
  matrix products  9.52 us (3%)
  other arithmetic  6.78 us (2%)
    psum x1, blocking collectives, shards(): lax.psum((partial_sum, jnp.sum(phi_keys, axis=0)), 'dom')  120 us
    psum x1, waiting for transfers between devices, shards(): lax.psum((partial_sum, jnp.sum(phi_keys, axis=0)), 'dom')  118 us
    all_to_all x1, blocking collectives, shards(): lax.all_to_all(mixed, 'head', split_axis=0, concat_axis=1, tiled=True)  20.3 us
    all_to_all x1, waiting for transfers between devices, list_the_windows(): z_new = lax.all_to_all(local_part, shard_axis, 0, 0)  12.4 us
    all_to_all x1, starting transfers between devices, list_the_windows(): z_new = lax.all_to_all(local_part, shard_axis, 0, 0)  10.5 us
  transfers between devices with their start and end apart: 4, of which 2 were waited for; matrix products, arithmetic and copies ran while one was open for 6% of the time, Pallas kernels for 0%

profile of v1, /device:TPU:1, one launch (start us, length us, event | category | flops | bytes accessed | tf_op | source)
XLA Modules:
  0.0 324.4 jit_solution(11955356980267230117)
XLA Ops:
  6.5 0.0 copy-start
  6.5 0.0 copy-start.6
  6.5 0.0 copy-start.1
  6.5 1.1 convert_reduce_fusion
  7.6 1.1 fusion.31
  8.7 1.0 fusion.33
  9.8 1.1 stack.2
  10.8 0.0 copy-start.7
  10.8 0.0 copy-start.5
  10.8 10.5 %all-to-all-start = ((bf16[8,128,512]{2,1,0:T(8,128)(2,1)}), bf16[8,128,512]{2,1,0:T(8,128)(2,1)S(1)}, u32[]{:S(2)}, u32[]{:S(2)}) async-start(bf16[8,128,512]{2,1,0:T(8,128)(2,1)} %stack.2), calls=%async_computation | async-start | bytes 2097152 | tf_op jit(solution)/shard_map/all_to_all | solution.py:16
  21.3 0.0 all-reduce.2.cloned.1.call-start
  21.3 0.0 copy-done.6
  21.3 0.6 compare_and_fusion
  21.9 0.1 reshape.304
  22.0 0.1 reshape.319
  22.1 0.0 copy-done.1
  22.1 0.0 copy-start.4
  22.1 0.8 gather_fusion
  22.9 0.1 reshape.303
  23.0 0.1 copy.20
  23.8 0.1 dynamic_slice.14
  23.9 0.1 select_bitcast_fusion
  23.9 0.0 copy-done.7
  23.9 0.1 fusion.44
  24.0 12.4 %all-to-all-done = bf16[8,128,512]{2,1,0:T(8,128)(2,1)S(1)} async-done(((bf16[8,128,512]{2,1,0:T(8,128)(2,1)}), bf16[8,128,512]{2,1,0:T(8,128)(2,1)S(1)}, u32[]{:S(2)}, u32[]{:S(2)}) %all-to-all-start) | async-done | bytes 1048608 | tf_op jit(solution)/shard_map/all_to_all | solution.py:16
  36.4 0.0 copy-done.5
  36.4 0.5 convolution_convert_fusion
  37.0 1.3 collective-permute-start
  38.3 1.3 collective-permute-start.1
  39.6 0.1 multiply_reduce_fusion
  39.7 0.0 copy-done.4
  39.7 1.3 fusion.48
  41.0 1.1 fusion.27
  42.1 1.1 fusion.12
  43.3 0.7 copy.30
  43.9 0.0 all-reduce.2.cloned.1.call-update
  44.0 120.2 %psum.15 = f32[256]{0:T(256)S(1)} all-reduce(f32[256]{0:T(256)S(1)} %get-tuple-element.43), channel_id=1, replica_groups=mesh['dom'=64,'head'=8] {'dom'}, use_global_device_ids=true, to_apply=%region_8.10 | all-reduce | flops 256 | bytes 2048 | tf_op jit(solution)/shard_map/psum | solution.py:79
  164.2 1.0 fusion.49
  165.1 0.0 collective-permute-done
  165.1 0.0 collective-permute-done.1
  165.1 0.1 maximum_bitcast_fusion
  165.2 0.2 copy.29
  165.4 0.1 fusion.47
  165.5 0.2 copy_bitcast_fusion
  165.6 0.7 gather_fusion.1
  166.4 0.7 gather_fusion.2
  167.1 1.8 broadcast_select_fusion
  168.8 0.6 copy.22
  169.4 0.0 copy-start.3
  169.4 0.9 reshape.272
  170.3 1.7 copy.19
  172.0 1.8 reshape.270
  173.8 0.0 copy-done.3
  173.8 0.0 copy-start.2
  173.8 0.7 fusion
  174.5 0.9 fusion.1
  175.4 0.0 copy-done.2
  175.4 1.0 fusion.24
  176.4 0.2 copy.24
  176.5 117.8 %all-reduce.2.cloned.1.call-done = f32[256,64]{0,1:T(8,128)} async-done(((f32[256,64]{0,1:T(8,128)}), f32[256,64]{0,1:T(8,128)}) %all-reduce.2.cloned.1.call-update) | async-done | bytes 65552 | tf_op jit(solution)/shard_map/psum | solution.py:79
  294.4 2.0 fusion.20
  296.4 20.3 %all_to_all.24 = bf16[8,128,64]{1,2,0:T(8,128)(2,1)S(1)} all-to-all(bf16[8,128,64]{1,2,0:T(8,128)(2,1)S(1)} %copy.26), channel_id=1, replica_groups=mesh['dom'=64,'head'=8] {'head'}, dimensions={0} | all-to-all | bytes 262144 | tf_op jit(solution)/shard_map/all_to_all | solution.py:132
  316.7 0.0 copy-done
  316.7 0.9 convolution_convert_fusion.1
  (13 shorter events, 0.1 us)
Async XLA Ops:
  6.5 310.1 %copy-start = (bf16[512,512]{1,0:T(8,128)(2,1)S(1)}, bf16[512,512]{1,0:T(8,128)(2,1)}, u32[]{:S(2)}) copy-start(bf16[512,512]{1,0:T(8,128)(2,1)} %param.14) | copy-start | bytes 1572868
  6.5 14.8 %copy-start.6 = (s32[8,6]{1,0:T(8,128)S(1)}, s32[8,6]{1,0:T(8,128)}, u32[]{:S(2)}) copy-start(s32[8,6]{1,0:T(8,128)} %param.17) | copy-start | bytes 580
  6.5 15.6 %copy-start.1 = (s32[512]{0:T(512)S(1)}, s32[512]{0:T(512)}, u32[]{:S(2)}) copy-start(s32[512]{0:T(512)} %param.19) | copy-start | bytes 6148
  10.8 13.1 %copy-start.7 = (s32[8]{0:T(128)S(1)}, s32[8]{0:T(128)}, u32[]{:S(2)}) copy-start(s32[8]{0:T(128)} %param.18) | copy-start | bytes 100
  10.8 25.6 %copy-start.5 = (bf16[512,192]{0,1:T(8,128)(2,1)S(1)}, bf16[512,192]{0,1:T(8,128)(2,1)}, u32[]{:S(2)}) copy-start(bf16[512,192]{0,1:T(8,128)(2,1)} %param.13) | copy-start | bytes 589828
  10.8 25.6 %all-to-all-start = ((bf16[8,128,512]{2,1,0:T(8,128)(2,1)}), bf16[8,128,512]{2,1,0:T(8,128)(2,1)S(1)}, u32[]{:S(2)}, u32[]{:S(2)}) async-start(bf16[8,128,512]{2,1,0:T(8,128)(2,1)} %stack.2), calls=%async_computation | async-start | bytes 2097152 | tf_op jit(solution)/shard_map/all_to_all | solution.py:16
  21.3 273.0 %all-reduce.2.cloned.1.call-start = ((), (), s32[]{:S(2)}) async-start(), calls=%async_computation.2 | async-start | bytes 131072 | tf_op jit(solution)/shard_map/psum | solution.py:79
  22.1 17.6 %copy-start.4 = (f32[1,64,256]{2,1,0:T(8,128)S(1)}, f32[1,64,256]{2,1,0:T(8,128)}, u32[]{:S(2)}) copy-start(f32[1,64,256]{2,1,0:T(8,128)} %param.15) | copy-start | bytes 196612
  37.0 128.2 %collective-permute-start = (bf16[1024,128]{0,1:T(8,128)(2,1)S(1)}, bf16[1024,128]{0,1:T(8,128)(2,1)S(1)}, u32[]{:S(2)}, u32[]{:S(2)}) collective-permute-start(bf16[1024,128]{0,1:T(8,128)(2,1)S(1)} %bitcast.150), channel_id=1, source_target_pairs={{0,8},{8,16},{16,24},{24,32},{32,40},{40,48},{48,56},{56,64},{64,7... | collective-permute-start | bytes 786440 | tf_op jit(solution)/shard_map/ppermute | solution.py:29
  38.3 126.9 %collective-permute-start.1 = (bf16[1024,128]{0,1:T(8,128)(2,1)S(1)}, bf16[1024,128]{0,1:T(8,128)(2,1)S(1)}, u32[]{:S(2)}, u32[]{:S(2)}) collective-permute-start(bf16[1024,128]{0,1:T(8,128)(2,1)S(1)} %bitcast.151), channel_id=1, source_target_pairs={{8,0},{16,8},{24,16},{32,24},{40,32},{48,40},{56,48},{64,56},{72,6... | collective-permute-start | bytes 786440 | tf_op jit(solution)/shard_map/ppermute | solution.py:32
  169.4 4.4 %copy-start.3 = (bf16[8,8,8,128]{3,2,1,0:T(8,128)(2,1)S(1)}, bf16[8,8,8,128]{3,2,1,0:T(8,128)(2,1)}, u32[]{:S(2)}) copy-start(bf16[8,8,8,128]{3,2,1,0:T(8,128)(2,1)} %copy.30) | copy-start | bytes 393220
  173.8 1.6 copy-start.2
Sparse Core Ops, SparseCore 0:
  44.1 250.2 all-reduce.1
